TPU v7x, 128 devices: a whole 4x4x4 slice. The times are simulated.
128 devices in a mesh: head: 8 (over z, y_lo), exp: 16 (over y_hi, x, core).
Axes of the slice: x: 4, y: 4 (y_hi: 2, y_lo: 2; y = y_hi * 2 + y_lo), z: 4, core: 2. Of those that a mesh axis runs over, the one named last changes fastest.
Arguments:
- k_pre: bfloat16 [8, 32, 128, 4096], P(None, 'exp', None, 'head'), may hold values from -6 to 6
- v_pre: bfloat16 [8, 32, 128, 4096], P(None, 'exp', None, 'head'), may hold values from -6 to 6
- pre_decay: float32 [8, 32, 128, 32], P(None, 'exp', None, 'head'), may hold values from -1 to 0, as said below
- q_dec: bfloat16 [8, 32, 4, 4096], P('head', 'exp'), may hold values from -6 to 6
- k_dec: bfloat16 [8, 32, 4, 4096], P('head', 'exp'), may hold values from -6 to 6
- v_dec: bfloat16 [8, 32, 4, 4096], P('head', 'exp'), may hold values from -6 to 6
- dec_decay: float32 [8, 32, 4, 32], P('head', 'exp'), may hold values from -1 to 0, as said below
- x_dec: bfloat16 [8, 32, 4, 6144], P('head', 'exp'), may hold values from -6 to 6
- route: int32 [8, 32, 4, 2], P('head', 'exp'), may hold values from 0 to 15, all different within a row; in each aligned block of 8 rows (0 to 7, 8 to 15, ..., all dimensions but the last counted through in order) at most 2 rows name the same one
- att_gain: float32 [4096], replicated, may hold values from 0.25 to 1.75
- w_o: bfloat16 [4096, 6144], P('exp'), may hold values from -0.09375 to 0.09375
- ffn_gain: float32 [6144], replicated, may hold values from 0.25 to 1.75
- w_router: bfloat16 [6144, 16], replicated, may hold values from -0.15625 to 0.15625
- w_in: bfloat16 [16, 6144, 5120], P('exp', None, 'head'), may hold values from -0.078125 to 0.078125
- w_out: bfloat16 [16, 5120, 6144], P('exp', 'head'), may hold values from -0.078125 to 0.078125
Outputs:
- decoded: bfloat16 [8, 32, 4, 6144], P('head', 'exp')
Inputs may be any that keep to these rules, and one draw needn't show every extreme that they name: `route`: each token names two different experts. In each aligned block of 8 tokens (the tokens of one device, in the order group, member, step) no expert is named by more than 2 tokens, a bound that some block reaches. `pre_decay`: log decay of a head at one token. `dec_decay`: log decay of a head at one step.
All inputs are finite; a program needn't handle non-finite values.
Results may differ from a plain program's by a relative error of at most 0.008.
Values may be sent and summed in bfloat16 or wider, within the bound.
No kernel may reach another device: no remote copies, remote signals or barrier semaphores. Data moves between devices by JAX's collectives and lax.ppermute only.
A program may use at most 128 MiB of HBM per device.

v0:
```python
import jax
import jax.numpy as jnp
from jax import lax
from jax.experimental import pallas as pl
from jax.experimental.pallas import tpu as pltpu
from jax.sharding import PartitionSpec as P

CAP = 2
EXTRA = 128
AXES = ("head", "exp")
F32 = jnp.float32
BF16 = jnp.bfloat16
HIGHEST = lax.Precision.HIGHEST


def device_pairs(move):
    pairs = []
    for head in range(8):
        for exp in range(16):
            to_head, to_exp = move(head, exp)
            pairs.append((head * 16 + exp, to_head * 16 + to_exp))
    return pairs


CORE = device_pairs(lambda head, exp: (head, exp ^ 1))
Y_LO = device_pairs(lambda head, exp: (head ^ 1, exp))
Z_UP = device_pairs(lambda head, exp: ((head + 2) % 8, exp))
Z_DOWN = device_pairs(lambda head, exp: ((head + 6) % 8, exp))
Z_FAR = device_pairs(lambda head, exp: ((head + 4) % 8, exp))
SWAP = device_pairs(lambda head, exp: (exp // 2, 2 * head + exp % 2))


def send(value, pairs):
    return lax.ppermute(value, AXES, pairs)


def split_two(value):
    high = lax.reduce_precision(value, 8, 7)
    return high.astype(BF16), (value - high).astype(BF16)


def whole(count):
    return [pl.BlockSpec(memory_space=pltpu.VMEM)] * count


def pack_kernel(
    queries_hbm,
    keys_hbm,
    values_hbm,
    decay_hbm,
    out_ref,
    queries_ref,
    keys_ref,
    values_ref,
    decay_ref,
    sems,
):
    sources = (queries_hbm, keys_hbm, values_hbm, decay_hbm)
    targets = (queries_ref, keys_ref, values_ref, decay_ref)
    copies = [
        pltpu.make_async_copy(source, target, sems.at[i])
        for i, (source, target) in enumerate(zip(sources, targets))
    ]
    for copy in copies:
        copy.start()
    for copy in copies:
        copy.wait()
    blocks, _, width = out_ref.shape
    members, steps = decay_ref.shape[1], decay_ref.shape[2]
    rows = []
    for member in range(members):
        running = decay_ref[0, member, 0:1]
        rows.append(running)
        for step in range(1, steps):
            running = running + decay_ref[0, member, step : step + 1]
            rows.append(running)
    summed = jnp.concatenate(rows, axis=0)
    count = members * steps
    heads = summed.shape[1]
    summed = jnp.concatenate([summed, jnp.zeros((count, 128 - heads), F32)], axis=1)
    high = summed.astype(BF16).astype(F32)
    rest = summed - high
    middle = rest.astype(BF16).astype(F32)
    pieces = [high, middle, rest - middle]
    if width > 384:
        pieces.append(jnp.zeros((count, width - 384), F32))
    decays = jnp.concatenate(pieces, axis=1)
    arrays = [
        jnp.concatenate([ref[0, m].astype(F32) for m in range(members)], axis=0)
        for ref in (queries_ref, keys_ref, values_ref)
    ]
    for block in range(blocks):
        lanes = slice(block * width, (block + 1) * width)
        out_ref[block] = jnp.concatenate(
            [array[:, lanes] for array in arrays] + [decays], axis=0
        ).astype(BF16)


def in_hbm(count):
    return [pl.BlockSpec(memory_space=pltpu.MemorySpace.HBM)] * count


def pin(*arrays):
    return [pltpu.with_memory_space_constraint(array, pltpu.MemorySpace.HBM) for array in arrays]


def pack_decode(q_dec, k_dec, v_dec, dec_decay, blocks):
    members, steps, width = q_dec.shape[1:]
    return pl.pallas_call(
        pack_kernel,
        in_specs=in_hbm(4),
        out_specs=whole(1)[0],
        out_shape=pltpu.HBM((blocks, 4 * members * steps, width // blocks), BF16),
        scratch_shapes=[pltpu.VMEM(array.shape, array.dtype) for array in (q_dec, k_dec, v_dec, dec_decay)]
        + [pltpu.SemaphoreType.DMA((4,))],
        compiler_params=pltpu.CompilerParams(vmem_limit_bytes=6 << 20),
    )(*pin(q_dec, k_dec, v_dec, dec_decay))


def readout_kernel(
    keys_hbm,
    values_hbm,
    decay_hbm,
    gain_hbm,
    dec_ref,
    out_ref,
    keys_ref,
    values_ref,
    decay_ref,
    gain_ref,
    sems,
):
    groups, members = keys_ref.shape[0], keys_ref.shape[1]
    heads = decay_ref.shape[2]
    length = decay_ref.shape[3]
    width = keys_ref.shape[3]
    head_dim = width // heads
    rows_per_head = dec_ref.shape[1] // 4
    steps = rows_per_head // members
    rows = heads * rows_per_head
    head_id = lax.axis_index("head")
    decay_copy = pltpu.make_async_copy(decay_hbm, decay_ref, sems.at[2 * groups])
    decay_copy.start()
    gain_copy = pltpu.make_async_copy(gain_hbm, gain_ref, sems.at[2 * groups + 1])
    gain_copy.start()
    copies = []
    for group in range(groups):
        copies.append(
            (
                pltpu.make_async_copy(keys_hbm.at[group], keys_ref.at[group], sems.at[group]),
                pltpu.make_async_copy(
                    values_hbm.at[group], values_ref.at[group], sems.at[groups + group]
                ),
            )
        )
        for copy in copies[-1]:
            copy.start()
    earlier = lax.broadcasted_iota(jnp.int32, (length, length), 0)
    later = lax.broadcasted_iota(jnp.int32, (length, length), 1)
    after = (earlier > later).astype(F32)
    row = lax.broadcasted_iota(jnp.int32, (rows, width), 0)
    lane = lax.broadcasted_iota(jnp.int32, (rows, width), 1)
    own_head = (row // rows_per_head) == (lane // head_dim)
    row_s = lax.broadcasted_iota(jnp.int32, (rows, length), 0)
    row_d = lax.broadcasted_iota(jnp.int32, (rows, rows_per_head), 0) % rows_per_head
    col_d = lax.broadcasted_iota(jnp.int32, (rows, rows_per_head), 1)
    causal = ((row_d // steps) == (col_d // steps)) & ((col_d % steps) <= (row_d % steps))
    extra_lane = lax.broadcasted_iota(jnp.int32, (rows_per_head, EXTRA), 1)
    decay_copy.wait()
    gain_copy.wait()
    gain = gain_ref[:, pl.ds(pl.multiple_of(head_id * width, width), width)]
    summed = jnp.concatenate(
        [decay_ref[g, m] for g in range(groups) for m in range(members)], axis=0
    )
    factors = jnp.exp(jnp.dot(summed, after, precision=HIGHEST, preferred_element_type=F32))

    half = groups // 2
    for start in (0, half):
        span = range(start, start + half)
        cums, spreads, blocks = {}, {}, {}
        for group in span:
            block = dec_ref[group].astype(F32)
            blocks[group] = block
            parts = block[3 * rows_per_head : 4 * rows_per_head]
            all_cum = parts[:, 0:128] + parts[:, 128:256] + parts[:, 256:384]
            cums[group] = jnp.concatenate(
                [
                    jnp.broadcast_to(
                        jnp.sum(
                            jnp.where(extra_lane == head_id * heads + h, all_cum, 0.0),
                            axis=1,
                            keepdims=True,
                        ),
                        (rows_per_head, head_dim),
                    )
                    for h in range(heads)
                ],
                axis=1,
            )
            queries = jnp.concatenate([block[0:rows_per_head]] * heads, axis=0)
            spreads[group] = jnp.where(own_head, queries, 0.0).astype(BF16)
        for group in span:
            for copy in copies[group]:
                copy.wait()
        pairs = [(group, member) for group in span for member in range(members)]
        scores = {
            (group, member): lax.dot_general(
                spreads[group],
                keys_ref[group, member],
                (((1,), (1,)), ((), ())),
                preferred_element_type=F32,
            )
            for group, member in pairs
        }
        near = {
            group: lax.dot_general(
                spreads[group],
                blocks[group][rows_per_head : 2 * rows_per_head].astype(BF16),
                (((1,), (1,)), ((), ())),
                preferred_element_type=F32,
            )
            for group in span
        }
        weighed = {}
        for group, member in pairs:
            first = (group * members + member) * heads
            factor = jnp.concatenate(
                [
                    jnp.broadcast_to(factors[first + h : first + h + 1], (rows_per_head, length))
                    for h in range(heads)
                ],
                axis=0,
            )
            score = scores[group, member] * factor
            score = jnp.where((row_s % rows_per_head) // steps == member, score, 0.0)
            high = score.astype(BF16)
            low = (score - high.astype(F32)).astype(BF16)
            weighed[group, member] = jnp.concatenate([high, low], axis=0)
        sums = {
            (group, member): jnp.dot(
                weighed[group, member], values_ref[group, member], preferred_element_type=F32
            )
            for group, member in pairs
        }
        results = []
        for group in span:
            cum = cums[group]
            values = blocks[group][2 * rows_per_head : 3 * rows_per_head] * jnp.exp(-cum)
            total = jnp.dot(
                jnp.where(causal, near[group], 0.0),
                values,
                precision=HIGHEST,
                preferred_element_type=F32,
            )
            for member in range(members):
                both = sums[group, member]
                total = total + both[:rows] + both[rows:]
            total = jnp.where(own_head, total, 0.0)
            readout = total[0:rows_per_head]
            for h in range(1, heads):
                readout = readout + total[h * rows_per_head : (h + 1) * rows_per_head]
            readout = readout * jnp.exp(cum) * (1.0 / head_dim)
            squares = jnp.sum(readout * readout, axis=1, keepdims=True)
            high = squares.astype(BF16).astype(F32)
            extra = jnp.where(
                extra_lane == 0, high, jnp.where(extra_lane == 1, squares - high, 0.0)
            )
            results.append(jnp.concatenate([readout * gain, extra], axis=1))
        at = slice(start * rows_per_head, (start + half) * rows_per_head)
        out_ref[at, :] = jnp.concatenate(results, axis=0).astype(BF16)


def readout_features(k_pre, v_pre, decay, dec, gain):
    groups, members, length, width = k_pre.shape
    count = groups * dec.shape[1] // 4
    return pl.pallas_call(
        readout_kernel,
        in_specs=in_hbm(4) + whole(1),
        out_specs=whole(1)[0],
        out_shape=jax.ShapeDtypeStruct((count, width + EXTRA), BF16),
        scratch_shapes=[
            pltpu.VMEM(k_pre.shape, BF16),
            pltpu.VMEM(v_pre.shape, BF16),
            pltpu.VMEM(decay.shape, F32),
            pltpu.VMEM(gain.shape, F32),
            pltpu.SemaphoreType.DMA((2 * groups + 2,)),
        ],
        compiler_params=pltpu.CompilerParams(vmem_limit_bytes=14 << 20),
        cost_estimate=pl.CostEstimate(
            flops=2 * 2 * 64 * groups * members * length * width,
            bytes_accessed=4 * groups * members * length * width,
            transcendentals=0,
        ),
    )(*pin(k_pre, v_pre, decay, gain), dec)


def stage_kernel(source_hbm, out_ref, sems):
    pieces = sems.shape[0]
    rows = out_ref.shape[0] // pieces
    copies = [
        pltpu.make_async_copy(
            source_hbm.at[pl.ds(i * rows, rows)], out_ref.at[pl.ds(i * rows, rows)], sems.at[i]
        )
        for i in range(pieces)
    ]
    for copy in copies:
        copy.start()
    for copy in copies:
        copy.wait()


def stage(weights):
    return pl.pallas_call(
        stage_kernel,
        in_specs=in_hbm(1),
        out_specs=whole(1)[0],
        out_shape=jax.ShapeDtypeStruct(weights.shape, weights.dtype),
        scratch_shapes=[pltpu.SemaphoreType.DMA((4,))],
        compiler_params=pltpu.CompilerParams(vmem_limit_bytes=2 << 20),
        cost_estimate=pl.CostEstimate(
            flops=0, bytes_accessed=2 * weights.size * 2, transcendentals=0
        ),
    )(*pin(weights))


def project_kernel(features_ref, own_ref, other_ref, out_ref):
    half, model_dim = own_ref.shape
    first = lax.axis_index("exp") % 2 == 0
    low, high = features_ref[:, 0:half], features_ref[:, half : 2 * half]
    mine = jnp.where(first, low, high)
    theirs = jnp.where(first, high, low)
    piece = model_dim // 2
    for at in (slice(0, piece), slice(piece, model_dim)):
        out_ref[:, at] = (
            jnp.dot(mine, own_ref[:, at], preferred_element_type=F32)
            + jnp.dot(theirs, other_ref[:, at], preferred_element_type=F32)
        ).astype(BF16)
    out_ref[:, model_dim:] = features_ref[:, 2 * half : 2 * half + EXTRA]


def project(features, own, other):
    count = features.shape[0]
    half, model_dim = own.shape
    return pl.pallas_call(
        project_kernel,
        in_specs=whole(3),
        out_specs=whole(1)[0],
        out_shape=pltpu.HBM((count, model_dim + EXTRA), BF16),
        compiler_params=pltpu.CompilerParams(vmem_limit_bytes=8 << 20),
        cost_estimate=pl.CostEstimate(
            flops=4 * count * half * model_dim,
            bytes_accessed=4 * half * model_dim,
            transcendentals=0,
        ),
    )(features, own, other)


def inward_kernel(rows_ref, w_in_ref, hidden_ref):
    depth = rows_ref.shape[1] // 2
    total = jnp.dot(rows_ref[:, :depth], w_in_ref[:depth, :], preferred_element_type=F32)
    hidden_ref[...] = total
    hidden_ref[...] += jnp.dot(rows_ref[:, depth:], w_in_ref[depth:, :], preferred_element_type=F32)


def inward(rows, w_in):
    count, model_dim = rows.shape
    hidden = w_in.shape[1]
    return pl.pallas_call(
        inward_kernel,
        in_specs=whole(2),
        out_specs=whole(1)[0],
        out_shape=pltpu.VMEM((count, hidden), F32),
        compiler_params=pltpu.CompilerParams(vmem_limit_bytes=6 << 20),
        cost_estimate=pl.CostEstimate(
            flops=2 * count * model_dim * hidden,
            bytes_accessed=2 * model_dim * hidden + 2 * count * model_dim,
            transcendentals=0,
        ),
    )(rows, w_in)


def middle_kernel(early_ref, rows_ref, order_ref, w_in_ref, w_out_ref, active_ref, *last_refs):
    late = jnp.dot(rows_ref[...], w_in_ref[...], preferred_element_type=F32)
    hidden = jnp.concatenate([early_ref[...], late], axis=0)
    active = (hidden * jax.nn.sigmoid(hidden)).astype(BF16)
    active = jnp.dot(order_ref[...], active, preferred_element_type=F32).astype(BF16)
    active_ref[...] = active
    write_blocks(active[early_ref.shape[0] :], w_out_ref, last_refs, 2)


def write_blocks(active, w_out_ref, refs, pieces):
    rows, model_dim = refs[0].shape
    piece = model_dim // pieces
    for i in range(pieces):
        at = slice(i * piece, (i + 1) * piece)
        result = jnp.dot(active, w_out_ref[:, at], preferred_element_type=F32)
        for j, ref in enumerate(refs):
            ref[:, at] = result[j * rows : (j + 1) * rows].astype(BF16)


def middle(early, rows, order, w_in, w_out, block):
    count, model_dim = rows.shape
    hidden = w_in.shape[1]
    total = early.shape[0] + count
    return pl.pallas_call(
        middle_kernel,
        in_specs=whole(5),
        out_specs=whole(1 + count // block),
        out_shape=[pltpu.VMEM((total, hidden), BF16)]
        + [pltpu.VMEM((block, model_dim), BF16)] * (count // block),
        compiler_params=pltpu.CompilerParams(vmem_limit_bytes=8 << 20),
        cost_estimate=pl.CostEstimate(
            flops=4 * count * model_dim * hidden,
            bytes_accessed=4 * model_dim * hidden,
            transcendentals=total * hidden,
        ),
    )(early, rows, order, w_in, w_out)


def outward_kernel(active_ref, w_out_ref, *out_refs):
    rows = len(out_refs) * out_refs[0].shape[0]
    write_blocks(active_ref[0:rows, :], w_out_ref, out_refs, 3)


def outward(active, w_out, blocks, block):
    hidden, model_dim = w_out.shape
    count = blocks * block
    return pl.pallas_call(
        outward_kernel,
        in_specs=whole(2),
        out_specs=whole(blocks),
        out_shape=[pltpu.VMEM((block, model_dim), BF16)] * blocks,
        compiler_params=pltpu.CompilerParams(vmem_limit_bytes=8 << 20),
        cost_estimate=pl.CostEstimate(
            flops=2 * count * model_dim * hidden,
            bytes_accessed=2 * model_dim * hidden + 2 * count * model_dim,
            transcendentals=0,
        ),
    )(active, w_out)


def gather_heads(own, w_in, w_out, aside):
    own, w_in, w_out = lax.optimization_barrier((own, w_in, w_out))
    from_down = send(own, Z_UP)
    from_up = send(own, Z_DOWN)
    far = send(own, Z_FAR)
    beside = send(own, Y_LO)
    w_in, w_out = stage(w_in), stage(w_out)
    aside = send(aside, SWAP)
    beside, far, aside = lax.optimization_barrier((beside, far, aside))
    beside_down = send(beside, Z_UP)
    beside_up = send(beside, Z_DOWN)
    beside_far = send(far, Y_LO)
    early = inward(jnp.concatenate([own, from_up, from_down, far, beside]), w_in)
    late = jnp.concatenate([beside_up, beside_down, beside_far])
    return early, late, w_in, w_out, aside


def sum_kernel(*refs):
    total = refs[0][...].astype(F32)
    for ref in refs[1:-1]:
        total = total + ref[...].astype(F32)
    refs[-1][...] = total.astype(BF16)


def add(*arrays):
    return pl.pallas_call(
        sum_kernel,
        in_specs=whole(len(arrays)),
        out_specs=whole(1)[0],
        out_shape=pltpu.VMEM(arrays[0].shape, BF16),
        compiler_params=pltpu.CompilerParams(vmem_limit_bytes=4 << 20),
    )(*arrays)


def last_sum_kernel(*refs):
    out_ref = refs[-1]
    total = refs[0][...].astype(F32)
    for ref in refs[1:-1]:
        total = total + ref[...].astype(F32)
    for i in range(out_ref.shape[0]):
        out_ref[i] = total[CAP * i : CAP * (i + 1)].astype(BF16)


def scatter_heads(own, up, down, far, beside, beside_up, beside_down, beside_far):
    rows, width = own.shape
    first = send(beside_up, Z_UP)
    second = send(beside_down, Z_DOWN)
    third = send(beside_far, Y_LO)
    from_far = send(add(far, third), Z_FAR)
    from_down = send(up, Z_UP)
    from_up = send(down, Z_DOWN)
    from_beside = send(add(beside, first, second), Y_LO)
    return pl.pallas_call(
        last_sum_kernel,
        in_specs=whole(5),
        out_specs=whole(1)[0],
        out_shape=pltpu.HBM((rows // CAP, CAP, width), BF16),
        compiler_params=pltpu.CompilerParams(vmem_limit_bytes=6 << 20),
        cost_estimate=pl.CostEstimate(
            flops=0, bytes_accessed=12 * rows * width, transcendentals=0
        ),
    )(own, from_down, from_up, from_far, from_beside)


def finish_kernel(returned_ref, resid_ref, weights_ref, out_ref):
    members, steps, width = out_ref.shape[1:]
    tokens = members * steps
    slots = weights_ref.shape[1]
    copies = returned_ref.shape[0] // slots
    piece = width // 4
    for i in range(4):
        at = slice(i * piece, (i + 1) * piece)
        total = returned_ref[0:slots, at].astype(F32)
        for copy in range(1, copies):
            total = total + returned_ref[copy * slots : (copy + 1) * slots, at].astype(F32)
        mixed = jnp.dot(weights_ref[...], total.astype(BF16), preferred_element_type=F32)
        mixed = mixed[:tokens] + mixed[tokens:]
        decoded = resid_ref[:, at].astype(F32) + mixed
        for member in range(members):
            out_ref[0, member, :, at] = decoded[member * steps : (member + 1) * steps].astype(BF16)


def finish(returned, resid, weights, members, steps, width):
    return pl.pallas_call(
        finish_kernel,
        in_specs=whole(3),
        out_specs=whole(1)[0],
        out_shape=jax.ShapeDtypeStruct((1, members, steps, width), BF16),
        compiler_params=pltpu.CompilerParams(vmem_limit_bytes=6 << 20),
    )(returned, resid, weights)


def on_device(
    k_pre,
    v_pre,
    pre_decay,
    q_dec,
    k_dec,
    v_dec,
    dec_decay,
    x_dec,
    route,
    att_gain,
    w_o,
    ffn_gain,
    w_router,
    w_in,
    w_out,
):
    head_id = lax.axis_index("head")
    n_head, n_exp = lax.axis_size("head"), lax.axis_size("exp")
    owned, steps, width = q_dec.shape[1:]
    tokens = owned * steps
    model_dim = x_dec.shape[3]

    w_o_other = send(w_o, CORE)

    packed = pack_decode(q_dec, k_dec, v_dec, dec_decay, n_head)
    packed = lax.all_to_all(packed, "head", split_axis=0, concat_axis=0, tiled=True)
    features = readout_features(
        k_pre, v_pre, jnp.transpose(pre_decay, (0, 1, 3, 2)), packed, att_gain[None]
    )

    ids = route.reshape(tokens, 2)
    carried = jnp.concatenate(
        [
            x_dec.reshape(tokens, model_dim),
            jnp.pad(ids.astype(BF16), ((0, 0), (0, EXTRA - 2))),
        ],
        axis=1,
    )
    features, carried, w_o_other = lax.optimization_barrier((features, carried, w_o_other))
    features = send(features, SWAP)
    carried = send(carried, SWAP)
    x_here = carried[:, :model_dim]
    ids_here = carried[:, model_dim : model_dim + 2].astype(jnp.int32)
    w_o_other = stage(w_o_other)
    partial_sum = project(features, w_o, w_o_other)
    partial_sum = partial_sum.reshape(n_head, tokens, model_dim + EXTRA)
    parts = lax.all_to_all(
        partial_sum,
        "exp",
        split_axis=0,
        concat_axis=0,
        tiled=True,
        axis_index_groups=[list(range(c, n_exp, 2)) for c in range(2)],
    )
    summed = jnp.sum(parts.astype(F32), axis=0)
    squares = summed[:, model_dim : model_dim + 1] + summed[:, model_dim + 1 : model_dim + 2]
    attn = summed[:, :model_dim] * lax.rsqrt(squares / width + 1e-06)
    resid = (x_here.astype(F32) + attn).astype(BF16)
    resid_f = resid.astype(F32)
    mean_square = jnp.mean(resid_f * resid_f, axis=-1, keepdims=True)
    ffn_in = (resid_f * lax.rsqrt(mean_square + 1e-06) * ffn_gain).astype(BF16)

    experts = w_router.shape[1]
    logits = jnp.dot(ffn_in, w_router, preferred_element_type=F32)

    def slots_of(expert_ids):
        flat_ids = expert_ids.reshape(-1)
        order = jnp.arange(flat_ids.shape[0], dtype=jnp.int32)
        earlier = (flat_ids[:, None] == flat_ids[None, :]) & (order[:, None] > order[None, :])
        slots = jnp.sum(earlier.astype(jnp.int32), axis=1)
        target = (flat_ids * CAP + slots).reshape(tokens, 2)
        places = jnp.arange(experts * CAP, dtype=jnp.int32)
        return places[None, None, :] == target[:, :, None]

    table = jnp.sum(slots_of(ids_here).astype(F32), axis=1).astype(BF16)
    rows = jnp.dot(table.T, ffn_in, preferred_element_type=F32).astype(BF16)
    rows = rows.reshape(n_exp, CAP, model_dim)
    onehot = (ids_here[:, :, None] == jnp.arange(experts, dtype=jnp.int32)).astype(F32)
    gates = jax.nn.sigmoid(jnp.sum(onehot * logits[:, None, :], axis=-1))
    weights = gates / jnp.sum(gates, axis=-1, keepdims=True)
    weight_parts = jnp.concatenate(split_two(weights), axis=1)

    rows = lax.all_to_all(rows, "exp", split_axis=0, concat_axis=0, tiled=True)
    back = jnp.concatenate([resid, jnp.pad(weight_parts, ((0, 0), (0, EXTRA - 4)))], axis=1)
    early, late, near_in, near_out, back = gather_heads(
        rows.reshape(n_exp * CAP, model_dim), w_in[0], w_out[0], back
    )

    count = n_head * n_exp * CAP
    per_group = count // n_head // n_head
    offsets = jnp.array([0, 2, 6, 4, 1, 3, 7, 5], jnp.int32)

    def position(relative):
        step = offsets[relative]
        return ((head_id // 2 + step // 2) % 4) * 2 + (head_id % 2 + step % 2) % 2

    leaving = jnp.arange(count, dtype=jnp.int32)
    block = n_head * per_group
    goes_to = position(leaving // block)
    came_from = (leaving % block) // per_group
    key_out = (came_from * n_head + goes_to) * per_group + leaving % per_group
    key_in = (position(leaving // block) * n_head + (leaving % block) // per_group) * per_group
    key_in = key_in + leaving % per_group
    order = (key_out[:, None] == key_in[None, :]).astype(BF16)
    active, *last = middle(early, late, order, near_in, near_out, block)
    outputs = scatter_heads(*outward(active, near_out, early.shape[0] // block, block), *last)
    returned = lax.all_to_all(
        outputs, "exp", split_axis=0, concat_axis=0, tiled=True
    ).reshape(n_exp * CAP, model_dim)

    weights_here = back[:, model_dim : model_dim + 2].astype(F32)
    weights_here = weights_here + back[:, model_dim + 2 : model_dim + 4].astype(F32)
    spread = jnp.sum(slots_of(ids).astype(F32) * weights_here[:, :, None], axis=1)
    spread = jnp.concatenate(split_two(spread), axis=0)
    return finish(returned, back, spread, owned, steps, model_dim)


def solution(mesh):
    return jax.shard_map(
        on_device,
        mesh=mesh,
        in_specs=(
            P(None, "exp", None, "head"),
            P(None, "exp", None, "head"),
            P(None, "exp", None, "head"),
            P("head", "exp", None, None),
            P("head", "exp", None, None),
            P("head", "exp", None, None),
            P("head", "exp", None, None),
            P("head", "exp", None, None),
            P("head", "exp", None, None),
            P(),
            P("exp", None),
            P(),
            P(),
            P("exp", None, "head"),
            P("exp", "head", None),
        ),
        out_specs=P("head", "exp", None, None),
        check_vma=False,
    )
```

profile of v0, /device:TPU:1, one launch (start us, length us, event | category | flops | bytes accessed | tf_op | source)
XLA Modules:
  0.0 153.4 jit_solution(3385283895360805788)
XLA Ops:
  3.1 6.1 %all-to-all-start = ((bf16[8,32,512]{2,1,0:T(8,128)(2,1)}), bf16[8,32,512]{2,1,0:T(8,128)(2,1)S(1)}, u32[]{:S(2)}, u32[]{:S(2)}) async-start(bf16[8,32,512]{2,1,0:T(8,128)(2,1)} %shard_map.154), calls=%async_computation | async-start | bytes 524288 | tf_op jit(solution)/shard_map/all_to_all | solution.py:560
  11.2 5.2 %all-to-all-done.dec_ref = bf16[8,32,512]{2,1,0:T(8,128)(2,1)S(1)} async-done(((bf16[8,32,512]{2,1,0:T(8,128)(2,1)}), bf16[8,32,512]{2,1,0:T(8,128)(2,1)S(1)}, u32[]{:S(2)}, u32[]{:S(2)}) %all-to-all-start) | async-done | bytes 262176 | tf_op jit(solution)/shard_map/all_to_all | solution.py:560
  16.3 3.7 %shard_map.155 = bf16[64,640]{1,0:T(8,128)(2,1)S(1)} custom-call(bf16[8,2,128,512]{3,2,1,0:T(8,128)(2,1)} %keys_hbm.3, bf16[8,2,128,512]{3,2,1,0:T(8,128)(2,1)} %values_hbm.3, f32[8,2,4,128]{3,2,1,0:T(4,128)} %bitcast.14, f32[1,4096]{1,0:T(1,128)} %bitcast.15, bf16[8,32,512]{2,1,0:T(8,128)(2,1)S(1)} %all-to-all-done.dec_ref), custom_call_target="tpu_custom_call" | custom-call | flops 268435456 | bytes 4194304 | tf_op jit(solution)/shard_map/pallas_call | solution.py:276
  20.7 2.0 %shard_map.156.other_ref = bf16[256,6144]{1,0:T(8,128)(2,1)S(1)} custom-call(bf16[256,6144]{1,0:T(8,128)(2,1)} %collective-permute-done.source_hbm), custom_call_target="tpu_custom_call" | custom-call | bytes 6291456 | tf_op jit(solution)/shard_map/pallas_call | solution.py:313
  23.6 2.1 %shard_map.157 = bf16[64,6272]{1,0:T(8,128)(2,1)} custom-call(bf16[64,640]{1,0:T(8,128)(2,1)S(1)} %collective-permute-done.2.features_ref, bf16[256,6144]{1,0:T(8,128)(2,1)S(1)} %copy-done.1, bf16[256,6144]{1,0:T(8,128)(2,1)S(1)} %shard_map.156.other_ref), custom_call_target="tpu_custom_call" | custom-call | flops 402653184 | bytes 6291456 | tf_op jit(solution)/shard_map/pallas_call | solution.py:344
  25.7 16.4 %all-to-all-start.1 = ((bf16[8,8,6272]{2,1,0:T(8,128)(2,1)}), bf16[8,8,6272]{2,1,0:T(8,128)(2,1)S(1)}, u32[]{:S(2)}, u32[]{:S(2)}) async-start(bf16[8,8,6272]{2,1,0:T(8,128)(2,1)} %bitcast.13), calls=%async_computation.1 | async-start | bytes 1605632 | tf_op jit(solution)/shard_map/all_to_all | solution.py:581
  42.7 13.9 %all-to-all-done.1 = bf16[8,8,6272]{2,1,0:T(8,128)(2,1)S(1)} async-done(((bf16[8,8,6272]{2,1,0:T(8,128)(2,1)}), bf16[8,8,6272]{2,1,0:T(8,128)(2,1)S(1)}, u32[]{:S(2)}, u32[]{:S(2)}) %all-to-all-start.1) | async-done | bytes 802848 | tf_op jit(solution)/shard_map/all_to_all | solution.py:581
  59.3 4.2 %all-to-all-start.2 = ((bf16[16,2,6144]{2,1,0:T(2,128)(2,1)}), bf16[16,2,6144]{2,1,0:T(2,128)(2,1)S(1)}, u32[]{:S(2)}, u32[]{:S(2)}) async-start(bf16[16,2,6144]{2,1,0:T(2,128)(2,1)} %reshape.276), calls=%async_computation.2 | async-start | bytes 786432 | tf_op jit(solution)/shard_map/all_to_all | solution.py:617
  64.2 9.1 %all-to-all-done.2 = bf16[16,2,6144]{2,1,0:T(2,128)(2,1)S(1)} async-done(((bf16[16,2,6144]{2,1,0:T(2,128)(2,1)}), bf16[16,2,6144]{2,1,0:T(2,128)(2,1)S(1)}, u32[]{:S(2)}, u32[]{:S(2)}) %all-to-all-start.2) | async-done | bytes 393248 | tf_op jit(solution)/shard_map/all_to_all | solution.py:617
  75.3 3.3 %shard_map.158.w_in_ref = bf16[6144,640]{1,0:T(8,128)(2,1)S(1)} custom-call(bf16[6144,640]{1,0:T(8,128)(2,1)} %bitcast.11), custom_call_target="tpu_custom_call" | custom-call | bytes 15728640 | tf_op jit(solution)/shard_map/pallas_call | solution.py:313
  78.7 3.3 %shard_map.160.w_out_ref = bf16[640,6144]{1,0:T(8,128)(2,1)S(1)} custom-call(bf16[640,6144]{1,0:T(8,128)(2,1)} %bitcast.12), custom_call_target="tpu_custom_call" | custom-call | bytes 15728640 | tf_op jit(solution)/shard_map/pallas_call | solution.py:313
  82.2 4.3 %collective-permute-start.8 = (bf16[32,6144]{1,0:T(8,128)(2,1)S(1)}, bf16[32,6144]{1,0:T(8,128)(2,1)S(1)}, u32[]{:S(2)}, u32[]{:S(2)}) collective-permute-start(bf16[32,6144]{1,0:T(8,128)(2,1)S(1)} %collective-permute-done.5), channel_id=1, source_target_pairs={{0,96},{1,97},{2,98},{3,99},{4,100},{5,101},{6,102},{7,103},{8,104... | collective-permute-start | bytes 1179656 | tf_op jit(solution)/shard_map/ppermute | solution.py:34
  87.9 4.6 %collective-permute-done.3 = bf16[32,6144]{1,0:T(8,128)(2,1)S(1)} collective-permute-done((bf16[32,6144]{1,0:T(8,128)(2,1)S(1)}, bf16[32,6144]{1,0:T(8,128)(2,1)S(1)}, u32[]{:S(2)}, u32[]{:S(2)}) %collective-permute-start.3) | collective-permute-done | bytes 393248 | tf_op jit(solution)/shard_map/ppermute | solution.py:34
  92.5 1.9 %collective-permute-done.4 = bf16[32,6144]{1,0:T(8,128)(2,1)S(1)} collective-permute-done((bf16[32,6144]{1,0:T(8,128)(2,1)S(1)}, bf16[32,6144]{1,0:T(8,128)(2,1)S(1)}, u32[]{:S(2)}, u32[]{:S(2)}) %collective-permute-start.4) | collective-permute-done | bytes 393248 | tf_op jit(solution)/shard_map/ppermute | solution.py:34
  96.3 4.6 %collective-permute-done.8 = bf16[32,6144]{1,0:T(8,128)(2,1)S(1)} collective-permute-done((bf16[32,6144]{1,0:T(8,128)(2,1)S(1)}, bf16[32,6144]{1,0:T(8,128)(2,1)S(1)}, u32[]{:S(2)}, u32[]{:S(2)}) %collective-permute-start.8) | collective-permute-done | bytes 393248 | tf_op jit(solution)/shard_map/ppermute | solution.py:34
  102.6 3.1 %shard_map.161 = (bf16[256,640]{1,0:T(8,128)(2,1)S(1)}, bf16[32,6144]{1,0:T(8,128)(2,1)S(1)}, bf16[32,6144]{1,0:T(8,128)(2,1)S(1)}, bf16[32,6144]{1,0:T(8,128)(2,1)S(1)}) custom-call(f32[160,640]{1,0:T(8,128)S(1)} %shard_map.159.early_ref, bf16[96,6144]{1,0:T(8,128)(2,1)S(1)} %pad_maximum_fusion.rows_ref, ...), custom_call_target="tpu_custom_call" | custom-call | flops 1509949440 | bytes 15728640 | tf_op jit(solution)/shard_map/pallas_call | solution.py:405
  106.0 2.7 %collective-permute-start.16 = (bf16[32,6144]{1,0:T(8,128)(2,1)S(1)}, bf16[32,6144]{1,0:T(8,128)(2,1)S(1)}, u32[]{:S(2)}, u32[]{:S(2)}) collective-permute-start(bf16[32,6144]{1,0:T(8,128)(2,1)S(1)} %get-tuple-element.39), channel_id=1, source_target_pairs={{0,96},{1,97},{2,98},{3,99},{4,100},{5,101},{6,102},{7,103},{8,104... | collective-permute-start | bytes 1179656 | tf_op jit(solution)/shard_map/ppermute | solution.py:34
  109.7 2.5 %shard_map.162 = (bf16[32,6144]{1,0:T(8,128)(2,1)S(1)}, bf16[32,6144]{1,0:T(8,128)(2,1)}, bf16[32,6144]{1,0:T(8,128)(2,1)S(1)}, bf16[32,6144]{1,0:T(8,128)(2,1)S(1)}, bf16[32,6144]{1,0:T(8,128)(2,1)S(1)}) custom-call(bf16[256,640]{1,0:T(8,128)(2,1)S(1)} %get-tuple-element.31.active_ref, bf16[640,6144]{1,0:T(8,128)(2,1)S(1)} %shard_map.160.w_out_ref), custom_call_target="tpu_custom_call" | custom-call | flops 1258291200 | bytes 9830400 | tf_op jit(solution)/shard_map/pallas_call | solution.py:428
  112.2 2.7 %collective-permute-start.12 = (bf16[32,6144]{1,0:T(8,128)(2,1)S(1)}, bf16[32,6144]{1,0:T(8,128)(2,1)S(1)}, u32[]{:S(2)}, u32[]{:S(2)}) collective-permute-start(bf16[32,6144]{1,0:T(8,128)(2,1)S(1)} %get-tuple-element.34), channel_id=1, source_target_pairs={{0,96},{1,97},{2,98},{3,99},{4,100},{5,101},{6,102},{7,103},{8,104... | collective-permute-start | bytes 1179656 | tf_op jit(solution)/shard_map/ppermute | solution.py:34
  117.9 2.8 %collective-permute-start.14 = (bf16[32,6144]{1,0:T(8,128)(2,1)S(1)}, bf16[32,6144]{1,0:T(8,128)(2,1)S(1)}, u32[]{:S(2)}, u32[]{:S(2)}) collective-permute-start(bf16[32,6144]{1,0:T(8,128)(2,1)S(1)} %shard_map.163), channel_id=1, source_target_pairs={{0,64},{1,65},{2,66},{3,67},{4,68},{5,69},{6,70},{7,71},{8,72},{9,... | collective-permute-start | bytes 1179656 | tf_op jit(solution)/shard_map/ppermute | solution.py:34
  121.5 3.7 %collective-permute-done.11.refs_1_ = bf16[32,6144]{1,0:T(8,128)(2,1)S(1)} collective-permute-done((bf16[32,6144]{1,0:T(8,128)(2,1)}, bf16[32,6144]{1,0:T(8,128)(2,1)S(1)}, u32[]{:S(2)}, u32[]{:S(2)}) %collective-permute-start.11) | collective-permute-done | bytes 393248 | tf_op jit(solution)/shard_map/ppermute | solution.py:34
  125.1 9.3 %collective-permute-done.14.refs_3_ = bf16[32,6144]{1,0:T(8,128)(2,1)S(1)} collective-permute-done((bf16[32,6144]{1,0:T(8,128)(2,1)S(1)}, bf16[32,6144]{1,0:T(8,128)(2,1)S(1)}, u32[]{:S(2)}, u32[]{:S(2)}) %collective-permute-start.14) | collective-permute-done | bytes 393248 | tf_op jit(solution)/shard_map/ppermute | solution.py:34
  135.5 7.2 %all-to-all-start.3 = ((bf16[16,2,6144]{2,1,0:T(2,128)(2,1)}), bf16[16,2,6144]{2,1,0:T(2,128)(2,1)S(1)}, u32[]{:S(2)}, u32[]{:S(2)}) async-start(bf16[16,2,6144]{2,1,0:T(2,128)(2,1)} %shard_map.165), calls=%async_computation.3 | async-start | bytes 786432 | tf_op jit(solution)/shard_map/all_to_all | solution.py:641
  142.8 9.7 %all-to-all-done.3 = bf16[16,2,6144]{2,1,0:T(2,128)(2,1)S(1)} async-done(((bf16[16,2,6144]{2,1,0:T(2,128)(2,1)}), bf16[16,2,6144]{2,1,0:T(2,128)(2,1)S(1)}, u32[]{:S(2)}, u32[]{:S(2)}) %all-to-all-start.3) | async-done | bytes 393248 | tf_op jit(solution)/shard_map/all_to_all | solution.py:641
  (92 shorter events, 24.7 us)
Async XLA Ops:
  0.0 57.2 %copy-start = (bf16[6144,16]{0,1:T(8,128)(2,1)S(1)}, bf16[6144,16]{0,1:T(8,128)(2,1)}, u32[]{:S(2)}) copy-start(bf16[6144,16]{0,1:T(8,128)(2,1)} %param.28) | copy-start | bytes 589828
  0.0 20.0 %collective-permute-start = (bf16[256,6144]{1,0:T(8,128)(2,1)}, bf16[256,6144]{1,0:T(8,128)(2,1)}, u32[]{:S(2)}, u32[]{:S(2)}) collective-permute-start(bf16[256,6144]{1,0:T(8,128)(2,1)} %own_ref.1), channel_id=1, source_target_pairs={{0,1},{1,0},{2,3},{3,2},{4,5},{5,4},{6,7},{7,6},{8,9},{9,8},{10,11... | collective-permute-start | bytes 9437192 | tf_op jit(solution)/shard_map/ppermute | solution.py:34
  3.1 13.2 %all-to-all-start = ((bf16[8,32,512]{2,1,0:T(8,128)(2,1)}), bf16[8,32,512]{2,1,0:T(8,128)(2,1)S(1)}, u32[]{:S(2)}, u32[]{:S(2)}) async-start(bf16[8,32,512]{2,1,0:T(8,128)(2,1)} %shard_map.154), calls=%async_computation | async-start | bytes 524288 | tf_op jit(solution)/shard_map/all_to_all | solution.py:560
  20.0 3.4 %collective-permute-start.2 = (bf16[64,640]{1,0:T(8,128)(2,1)S(1)}, bf16[64,640]{1,0:T(8,128)(2,1)S(1)}, u32[]{:S(2)}, u32[]{:S(2)}) collective-permute-start(bf16[64,640]{1,0:T(8,128)(2,1)S(1)} %shard_map.155), channel_id=1, source_target_pairs={{0,0},{1,1},{2,16},{3,17},{4,32},{5,33},{6,48},{7,49},{8,64},{9,65... | collective-permute-start | bytes 245768 | tf_op jit(solution)/shard_map/ppermute | solution.py:34
  22.8 19.4 %collective-permute-start.1 = (bf16[8,6272]{1,0:T(8,128)(2,1)S(1)}, bf16[8,6272]{1,0:T(8,128)(2,1)S(1)}, u32[]{:S(2)}, u32[]{:S(2)}) collective-permute-start(bf16[8,6272]{1,0:T(8,128)(2,1)S(1)} %fusion.6), channel_id=1, source_target_pairs={{0,0},{1,1},{2,16},{3,17},{4,32},{5,33},{6,48},{7,49},{8,64},{9,65... | collective-permute-start | bytes 301064 | tf_op jit(solution)/shard_map/ppermute | solution.py:34
  25.7 31.6 %copy-start.2 = (f32[6144]{0:T(1024)S(1)}, f32[6144]{0:T(1024)}, u32[]{:S(2)}) copy-start(f32[6144]{0:T(1024)} %param.27) | copy-start | bytes 73732
  25.7 31.0 %all-to-all-start.1 = ((bf16[8,8,6272]{2,1,0:T(8,128)(2,1)}), bf16[8,8,6272]{2,1,0:T(8,128)(2,1)S(1)}, u32[]{:S(2)}, u32[]{:S(2)}) async-start(bf16[8,8,6272]{2,1,0:T(8,128)(2,1)} %bitcast.13), calls=%async_computation.1 | async-start | bytes 1605632 | tf_op jit(solution)/shard_map/all_to_all | solution.py:581
  59.3 14.1 %all-to-all-start.2 = ((bf16[16,2,6144]{2,1,0:T(2,128)(2,1)}), bf16[16,2,6144]{2,1,0:T(2,128)(2,1)S(1)}, u32[]{:S(2)}, u32[]{:S(2)}) async-start(bf16[16,2,6144]{2,1,0:T(2,128)(2,1)} %reshape.276), calls=%async_computation.2 | async-start | bytes 786432 | tf_op jit(solution)/shard_map/all_to_all | solution.py:617
  63.6 18.5 %collective-permute-start.7 = (bf16[8,6272]{1,0:T(8,128)(2,1)S(1)}, bf16[8,6272]{1,0:T(8,128)(2,1)S(1)}, u32[]{:S(2)}, u32[]{:S(2)}) collective-permute-start(bf16[8,6272]{1,0:T(8,128)(2,1)S(1)} %pad_maximum_fusion.1), channel_id=1, source_target_pairs={{0,0},{1,1},{2,16},{3,17},{4,32},{5,33},{6,48},{7,49},{8,64},{9,65... | collective-permute-start | bytes 301064 | tf_op jit(solution)/shard_map/ppermute | solution.py:34
  73.5 8.5 %collective-permute-start.5 = (bf16[32,6144]{1,0:T(8,128)(2,1)S(1)}, bf16[32,6144]{1,0:T(8,128)(2,1)S(1)}, u32[]{:S(2)}, u32[]{:S(2)}) collective-permute-start(bf16[32,6144]{1,0:T(8,128)(2,1)S(1)} %reshape.277), channel_id=1, source_target_pairs={{0,16},{1,17},{2,18},{3,19},{4,20},{5,21},{6,22},{7,23},{8,24},{9,... | collective-permute-start | bytes 1179656 | tf_op jit(solution)/shard_map/ppermute | solution.py:34
  73.6 8.6 %collective-permute-start.6 = (bf16[32,6144]{1,0:T(8,128)(2,1)S(1)}, bf16[32,6144]{1,0:T(8,128)(2,1)S(1)}, u32[]{:S(2)}, u32[]{:S(2)}) collective-permute-start(bf16[32,6144]{1,0:T(8,128)(2,1)S(1)} %reshape.277), channel_id=1, source_target_pairs={{0,64},{1,65},{2,66},{3,67},{4,68},{5,69},{6,70},{7,71},{8,72},{9,... | collective-permute-start | bytes 1179656 | tf_op jit(solution)/shard_map/ppermute | solution.py:34
  73.7 18.8 %collective-permute-start.3 = (bf16[32,6144]{1,0:T(8,128)(2,1)S(1)}, bf16[32,6144]{1,0:T(8,128)(2,1)S(1)}, u32[]{:S(2)}, u32[]{:S(2)}) collective-permute-start(bf16[32,6144]{1,0:T(8,128)(2,1)S(1)} %reshape.277), channel_id=1, source_target_pairs={{0,96},{1,97},{2,98},{3,99},{4,100},{5,101},{6,102},{7,103},{8,104... | collective-permute-start | bytes 1179656 | tf_op jit(solution)/shard_map/ppermute | solution.py:34
  74.9 19.5 %collective-permute-start.4 = (bf16[32,6144]{1,0:T(8,128)(2,1)S(1)}, bf16[32,6144]{1,0:T(8,128)(2,1)S(1)}, u32[]{:S(2)}, u32[]{:S(2)}) collective-permute-start(bf16[32,6144]{1,0:T(8,128)(2,1)S(1)} %reshape.277), channel_id=1, source_target_pairs={{0,32},{1,33},{2,34},{3,35},{4,36},{5,37},{6,38},{7,39},{8,40},{9,... | collective-permute-start | bytes 1179656 | tf_op jit(solution)/shard_map/ppermute | solution.py:34
  82.2 18.8 %collective-permute-start.8 = (bf16[32,6144]{1,0:T(8,128)(2,1)S(1)}, bf16[32,6144]{1,0:T(8,128)(2,1)S(1)}, u32[]{:S(2)}, u32[]{:S(2)}) collective-permute-start(bf16[32,6144]{1,0:T(8,128)(2,1)S(1)} %collective-permute-done.5), channel_id=1, source_target_pairs={{0,96},{1,97},{2,98},{3,99},{4,100},{5,101},{6,102},{7,103},{8,104... | collective-permute-start | bytes 1179656 | tf_op jit(solution)/shard_map/ppermute | solution.py:34
  86.5 16.1 %collective-permute-start.9 = (bf16[32,6144]{1,0:T(8,128)(2,1)S(1)}, bf16[32,6144]{1,0:T(8,128)(2,1)S(1)}, u32[]{:S(2)}, u32[]{:S(2)}) collective-permute-start(bf16[32,6144]{1,0:T(8,128)(2,1)S(1)} %collective-permute-done.5), channel_id=1, source_target_pairs={{0,32},{1,33},{2,34},{3,35},{4,36},{5,37},{6,38},{7,39},{8,40},{9,... | collective-permute-start | bytes 1179656 | tf_op jit(solution)/shard_map/ppermute | solution.py:34
  86.5 9.8 %collective-permute-start.10 = (bf16[32,6144]{1,0:T(8,128)(2,1)S(1)}, bf16[32,6144]{1,0:T(8,128)(2,1)S(1)}, u32[]{:S(2)}, u32[]{:S(2)}) collective-permute-start(bf16[32,6144]{1,0:T(8,128)(2,1)S(1)} %collective-permute-done.6), channel_id=1, source_target_pairs={{0,16},{1,17},{2,18},{3,19},{4,20},{5,21},{6,22},{7,23},{8,24},{9,... | collective-permute-start | bytes 1179656 | tf_op jit(solution)/shard_map/ppermute | solution.py:34
  105.7 11.0 %collective-permute-start.15 = (bf16[32,6144]{1,0:T(8,128)(2,1)S(1)}, bf16[32,6144]{1,0:T(8,128)(2,1)S(1)}, u32[]{:S(2)}, u32[]{:S(2)}) collective-permute-start(bf16[32,6144]{1,0:T(8,128)(2,1)S(1)} %get-tuple-element.38), channel_id=1, source_target_pairs={{0,32},{1,33},{2,34},{3,35},{4,36},{5,37},{6,38},{7,39},{8,40},{9,... | collective-permute-start | bytes 1179656 | tf_op jit(solution)/shard_map/ppermute | solution.py:34
  106.0 10.7 %collective-permute-start.16 = (bf16[32,6144]{1,0:T(8,128)(2,1)S(1)}, bf16[32,6144]{1,0:T(8,128)(2,1)S(1)}, u32[]{:S(2)}, u32[]{:S(2)}) collective-permute-start(bf16[32,6144]{1,0:T(8,128)(2,1)S(1)} %get-tuple-element.39), channel_id=1, source_target_pairs={{0,96},{1,97},{2,98},{3,99},{4,100},{5,101},{6,102},{7,103},{8,104... | collective-permute-start | bytes 1179656 | tf_op jit(solution)/shard_map/ppermute | solution.py:34
  108.6 9.1 %collective-permute-start.13 = (bf16[32,6144]{1,0:T(8,128)(2,1)S(1)}, bf16[32,6144]{1,0:T(8,128)(2,1)S(1)}, u32[]{:S(2)}, u32[]{:S(2)}) collective-permute-start(bf16[32,6144]{1,0:T(8,128)(2,1)S(1)} %get-tuple-element.36), channel_id=1, source_target_pairs={{0,16},{1,17},{2,18},{3,19},{4,20},{5,21},{6,22},{7,23},{8,24},{9,... | collective-permute-start | bytes 1179656 | tf_op jit(solution)/shard_map/ppermute | solution.py:34
  112.2 12.9 %collective-permute-start.11 = (bf16[32,6144]{1,0:T(8,128)(2,1)}, bf16[32,6144]{1,0:T(8,128)(2,1)S(1)}, u32[]{:S(2)}, u32[]{:S(2)}) collective-permute-start(bf16[32,6144]{1,0:T(8,128)(2,1)} %get-tuple-element.33), channel_id=1, source_target_pairs={{0,32},{1,33},{2,34},{3,35},{4,36},{5,37},{6,38},{7,39},{8,40},{9,... | collective-permute-start | bytes 1179656 | tf_op jit(solution)/shard_map/ppermute | solution.py:34
  112.2 12.9 %collective-permute-start.12 = (bf16[32,6144]{1,0:T(8,128)(2,1)S(1)}, bf16[32,6144]{1,0:T(8,128)(2,1)S(1)}, u32[]{:S(2)}, u32[]{:S(2)}) collective-permute-start(bf16[32,6144]{1,0:T(8,128)(2,1)S(1)} %get-tuple-element.34), channel_id=1, source_target_pairs={{0,96},{1,97},{2,98},{3,99},{4,100},{5,101},{6,102},{7,103},{8,104... | collective-permute-start | bytes 1179656 | tf_op jit(solution)/shard_map/ppermute | solution.py:34
  116.8 8.3 %collective-permute-start.17 = (bf16[32,6144]{1,0:T(8,128)(2,1)S(1)}, bf16[32,6144]{1,0:T(8,128)(2,1)S(1)}, u32[]{:S(2)}, u32[]{:S(2)}) collective-permute-start(bf16[32,6144]{1,0:T(8,128)(2,1)S(1)} %shard_map.164), channel_id=1, source_target_pairs={{0,16},{1,17},{2,18},{3,19},{4,20},{5,21},{6,22},{7,23},{8,24},{9,... | collective-permute-start | bytes 1179656 | tf_op jit(solution)/shard_map/ppermute | solution.py:34
  117.9 16.6 %collective-permute-start.14 = (bf16[32,6144]{1,0:T(8,128)(2,1)S(1)}, bf16[32,6144]{1,0:T(8,128)(2,1)S(1)}, u32[]{:S(2)}, u32[]{:S(2)}) collective-permute-start(bf16[32,6144]{1,0:T(8,128)(2,1)S(1)} %shard_map.163), channel_id=1, source_target_pairs={{0,64},{1,65},{2,66},{3,67},{4,68},{5,69},{6,70},{7,71},{8,72},{9,... | collective-permute-start | bytes 1179656 | tf_op jit(solution)/shard_map/ppermute | solution.py:34
  135.5 17.0 %all-to-all-start.3 = ((bf16[16,2,6144]{2,1,0:T(2,128)(2,1)}), bf16[16,2,6144]{2,1,0:T(2,128)(2,1)S(1)}, u32[]{:S(2)}, u32[]{:S(2)}) async-start(bf16[16,2,6144]{2,1,0:T(2,128)(2,1)} %shard_map.165), calls=%async_computation.3 | async-start | bytes 786432 | tf_op jit(solution)/shard_map/all_to_all | solution.py:641
  (2 other events, 11.3 us)
where the time goes:
time: 154 us; the launch traced here: 153 us
  waiting for transfers between devices  65.6 us (43%)
  starting transfers between devices  55.2 us (36%)
  Pallas kernels  25.6 us (17%)
  local copies, waits for them, and re-layouts  3.51 us (2%)
  other arithmetic  2.66 us (2%)
    ppermute x18, waiting for transfers between devices, send(): return lax.ppermute(value, AXES, pairs)  27.7 us
    ppermute x18, starting transfers between devices, send(): return lax.ppermute(value, AXES, pairs)  21.3 us
    all_to_all x1, starting transfers between devices, on_device(): lax.all_to_all(partial_sum, 'exp', split_axis=0, concat_axis=0, tiled=Tru...  16.4 us
    all_to_all x1, waiting for transfers between devices, on_device(): lax.all_to_all(partial_sum, 'exp', split_axis=0, concat_axis=0, tiled=Tru...  13.9 us
    all_to_all x1, waiting for transfers between devices, on_device(): lax.all_to_all(outputs, 'exp', split_axis=0, concat_axis=0, tiled=True)  9.69 us
    all_to_all x1, waiting for transfers between devices, on_device(): rows = lax.all_to_all(rows, 'exp', split_axis=0, concat_axis=0, tiled=True)  9.12 us
    pallas_call x3, Pallas kernels, stage(): pl.pallas_call(stage_kernel, in_specs=in_hbm(1), out_specs=whole(1)[0], o...  8.72 us
    all_to_all x1, starting transfers between devices, on_device(): lax.all_to_all(outputs, 'exp', split_axis=0, concat_axis=0, tiled=True)  7.2 us
  transfers between devices with their start and end apart: 22, of which 12 were waited for; matrix products, arithmetic and copies ran while one was open for 2% of the time, Pallas kernels for 13%

commit v1 on v0

--- a/solution.py
+++ b/solution.py
@@ -440,17 +440,18 @@
 
 
 def gather_heads(own, w_in, w_out, aside):
-    own, w_in, w_out = lax.optimization_barrier((own, w_in, w_out))
+    own, w_in = lax.optimization_barrier((own, w_in))
     from_down = send(own, Z_UP)
     from_up = send(own, Z_DOWN)
     far = send(own, Z_FAR)
     beside = send(own, Y_LO)
-    w_in, w_out = stage(w_in), stage(w_out)
+    w_in = stage(w_in)
     aside = send(aside, SWAP)
-    beside, far, aside = lax.optimization_barrier((beside, far, aside))
+    beside, far, aside, w_out = lax.optimization_barrier((beside, far, aside, w_out))
     beside_down = send(beside, Z_UP)
     beside_up = send(beside, Z_DOWN)
     beside_far = send(far, Y_LO)
+    w_out = stage(w_out)
     early = inward(jnp.concatenate([own, from_up, from_down, far, beside]), w_in)
     late = jnp.concatenate([beside_up, beside_down, beside_far])
     return early, late, w_in, w_out, aside

time: 154 us -> 154 us (level)
  transfers between devices with their start and end apart: 22 -> 22, of which waited for: 12 -> 13; matrix products, arithmetic and copies ran while one was open for 2% -> 2% of each run, Pallas kernels for 13% -> 13%
where the time goes in v1:
time: 154 us; the launch traced here: 153 us
  waiting for transfers between devices  65.4 us (42%)
  starting transfers between devices  55.4 us (36%)
  Pallas kernels  25.6 us (17%)
  local copies, waits for them, and re-layouts  3.51 us (2%)
  other arithmetic  2.66 us (2%)
    ppermute x18, waiting for transfers between devices, send(): return lax.ppermute(value, AXES, pairs)  27.5 us
    ppermute x18, starting transfers between devices, send(): return lax.ppermute(value, AXES, pairs)  21.3 us
    all_to_all x1, starting transfers between devices, on_device(): lax.all_to_all(partial_sum, 'exp', split_axis=0, concat_axis=0, tiled=Tru...  16.4 us
    all_to_all x1, waiting for transfers between devices, on_device(): lax.all_to_all(partial_sum, 'exp', split_axis=0, concat_axis=0, tiled=Tru...  13.9 us
    all_to_all x1, waiting for transfers between devices, on_device(): lax.all_to_all(outputs, 'exp', split_axis=0, concat_axis=0, tiled=True)  9.69 us
    all_to_all x1, waiting for transfers between devices, on_device(): rows = lax.all_to_all(rows, 'exp', split_axis=0, concat_axis=0, tiled=True)  9.12 us
    pallas_call x3, Pallas kernels, stage(): pl.pallas_call(stage_kernel, in_specs=in_hbm(1), out_specs=whole(1)[0], o...  8.72 us
    all_to_all x1, starting transfers between devices, on_device(): lax.all_to_all(outputs, 'exp', split_axis=0, concat_axis=0, tiled=True)  7.42 us
  transfers between devices with their start and end apart: 22, of which 13 were waited for; matrix products, arithmetic and copies ran while one was open for 2% of the time, Pallas kernels for 13%

profile of v1, /device:TPU:1, one launch (start us, length us, event | category | flops | bytes accessed | tf_op | source)
XLA Modules:
  0.0 153.4 jit_solution(2203013370239660458)
XLA Ops:
  3.1 6.1 %all-to-all-start = ((bf16[8,32,512]{2,1,0:T(8,128)(2,1)}), bf16[8,32,512]{2,1,0:T(8,128)(2,1)S(1)}, u32[]{:S(2)}, u32[]{:S(2)}) async-start(bf16[8,32,512]{2,1,0:T(8,128)(2,1)} %shard_map.154), calls=%async_computation | async-start | bytes 524288 | tf_op jit(solution)/shard_map/all_to_all | solution.py:561
  11.2 5.2 %all-to-all-done.dec_ref = bf16[8,32,512]{2,1,0:T(8,128)(2,1)S(1)} async-done(((bf16[8,32,512]{2,1,0:T(8,128)(2,1)}), bf16[8,32,512]{2,1,0:T(8,128)(2,1)S(1)}, u32[]{:S(2)}, u32[]{:S(2)}) %all-to-all-start) | async-done | bytes 262176 | tf_op jit(solution)/shard_map/all_to_all | solution.py:561
  16.3 3.7 %shard_map.155 = bf16[64,640]{1,0:T(8,128)(2,1)S(1)} custom-call(bf16[8,2,128,512]{3,2,1,0:T(8,128)(2,1)} %keys_hbm.3, bf16[8,2,128,512]{3,2,1,0:T(8,128)(2,1)} %values_hbm.3, f32[8,2,4,128]{3,2,1,0:T(4,128)} %bitcast.14, f32[1,4096]{1,0:T(1,128)} %bitcast.15, bf16[8,32,512]{2,1,0:T(8,128)(2,1)S(1)} %all-to-all-done.dec_ref), custom_call_target="tpu_custom_call" | custom-call | flops 268435456 | bytes 4194304 | tf_op jit(solution)/shard_map/pallas_call | solution.py:276
  20.7 2.0 %shard_map.156.other_ref = bf16[256,6144]{1,0:T(8,128)(2,1)S(1)} custom-call(bf16[256,6144]{1,0:T(8,128)(2,1)} %collective-permute-done.source_hbm), custom_call_target="tpu_custom_call" | custom-call | bytes 6291456 | tf_op jit(solution)/shard_map/pallas_call | solution.py:313
  23.6 2.1 %shard_map.157 = bf16[64,6272]{1,0:T(8,128)(2,1)} custom-call(bf16[64,640]{1,0:T(8,128)(2,1)S(1)} %collective-permute-done.2.features_ref, bf16[256,6144]{1,0:T(8,128)(2,1)S(1)} %copy-done.1, bf16[256,6144]{1,0:T(8,128)(2,1)S(1)} %shard_map.156.other_ref), custom_call_target="tpu_custom_call" | custom-call | flops 402653184 | bytes 6291456 | tf_op jit(solution)/shard_map/pallas_call | solution.py:344
  25.7 16.4 %all-to-all-start.1 = ((bf16[8,8,6272]{2,1,0:T(8,128)(2,1)}), bf16[8,8,6272]{2,1,0:T(8,128)(2,1)S(1)}, u32[]{:S(2)}, u32[]{:S(2)}) async-start(bf16[8,8,6272]{2,1,0:T(8,128)(2,1)} %bitcast.13), calls=%async_computation.1 | async-start | bytes 1605632 | tf_op jit(solution)/shard_map/all_to_all | solution.py:582
  42.7 13.9 %all-to-all-done.1 = bf16[8,8,6272]{2,1,0:T(8,128)(2,1)S(1)} async-done(((bf16[8,8,6272]{2,1,0:T(8,128)(2,1)}), bf16[8,8,6272]{2,1,0:T(8,128)(2,1)S(1)}, u32[]{:S(2)}, u32[]{:S(2)}) %all-to-all-start.1) | async-done | bytes 802848 | tf_op jit(solution)/shard_map/all_to_all | solution.py:582
  59.3 4.2 %all-to-all-start.2 = ((bf16[16,2,6144]{2,1,0:T(2,128)(2,1)}), bf16[16,2,6144]{2,1,0:T(2,128)(2,1)S(1)}, u32[]{:S(2)}, u32[]{:S(2)}) async-start(bf16[16,2,6144]{2,1,0:T(2,128)(2,1)} %reshape.276), calls=%async_computation.2 | async-start | bytes 786432 | tf_op jit(solution)/shard_map/all_to_all | solution.py:618
  64.2 9.1 %all-to-all-done.2 = bf16[16,2,6144]{2,1,0:T(2,128)(2,1)S(1)} async-done(((bf16[16,2,6144]{2,1,0:T(2,128)(2,1)}), bf16[16,2,6144]{2,1,0:T(2,128)(2,1)S(1)}, u32[]{:S(2)}, u32[]{:S(2)}) %all-to-all-start.2) | async-done | bytes 393248 | tf_op jit(solution)/shard_map/all_to_all | solution.py:618
  75.3 3.3 %shard_map.158.w_in_ref = bf16[6144,640]{1,0:T(8,128)(2,1)S(1)} custom-call(bf16[6144,640]{1,0:T(8,128)(2,1)} %bitcast.11), custom_call_target="tpu_custom_call" | custom-call | bytes 15728640 | tf_op jit(solution)/shard_map/pallas_call | solution.py:313
  82.2 4.3 %collective-permute-start.8 = (bf16[32,6144]{1,0:T(8,128)(2,1)S(1)}, bf16[32,6144]{1,0:T(8,128)(2,1)S(1)}, u32[]{:S(2)}, u32[]{:S(2)}) collective-permute-start(bf16[32,6144]{1,0:T(8,128)(2,1)S(1)} %collective-permute-done.5), channel_id=1, source_target_pairs={{0,96},{1,97},{2,98},{3,99},{4,100},{5,101},{6,102},{7,103},{8,104... | collective-permute-start | bytes 1179656 | tf_op jit(solution)/shard_map/ppermute | solution.py:34
  87.9 4.6 %collective-permute-done.3 = bf16[32,6144]{1,0:T(8,128)(2,1)S(1)} collective-permute-done((bf16[32,6144]{1,0:T(8,128)(2,1)S(1)}, bf16[32,6144]{1,0:T(8,128)(2,1)S(1)}, u32[]{:S(2)}, u32[]{:S(2)}) %collective-permute-start.3) | collective-permute-done | bytes 393248 | tf_op jit(solution)/shard_map/ppermute | solution.py:34
  92.5 1.9 %collective-permute-done.4 = bf16[32,6144]{1,0:T(8,128)(2,1)S(1)} collective-permute-done((bf16[32,6144]{1,0:T(8,128)(2,1)S(1)}, bf16[32,6144]{1,0:T(8,128)(2,1)S(1)}, u32[]{:S(2)}, u32[]{:S(2)}) %collective-permute-start.4) | collective-permute-done | bytes 393248 | tf_op jit(solution)/shard_map/ppermute | solution.py:34
  94.5 3.3 %shard_map.160.w_out_ref = bf16[640,6144]{1,0:T(8,128)(2,1)S(1)} custom-call(bf16[640,6144]{1,0:T(8,128)(2,1)} %bitcast.12), custom_call_target="tpu_custom_call" | custom-call | bytes 15728640 | tf_op jit(solution)/shard_map/pallas_call | solution.py:313
  102.6 3.1 %shard_map.161 = (bf16[256,640]{1,0:T(8,128)(2,1)S(1)}, bf16[32,6144]{1,0:T(8,128)(2,1)S(1)}, bf16[32,6144]{1,0:T(8,128)(2,1)S(1)}, bf16[32,6144]{1,0:T(8,128)(2,1)S(1)}) custom-call(f32[160,640]{1,0:T(8,128)S(1)} %shard_map.159.early_ref, bf16[96,6144]{1,0:T(8,128)(2,1)S(1)} %pad_maximum_fusion.rows_ref, ...), custom_call_target="tpu_custom_call" | custom-call | flops 1509949440 | bytes 15728640 | tf_op jit(solution)/shard_map/pallas_call | solution.py:405
  106.0 2.7 %collective-permute-start.16 = (bf16[32,6144]{1,0:T(8,128)(2,1)S(1)}, bf16[32,6144]{1,0:T(8,128)(2,1)S(1)}, u32[]{:S(2)}, u32[]{:S(2)}) collective-permute-start(bf16[32,6144]{1,0:T(8,128)(2,1)S(1)} %get-tuple-element.39), channel_id=1, source_target_pairs={{0,96},{1,97},{2,98},{3,99},{4,100},{5,101},{6,102},{7,103},{8,104... | collective-permute-start | bytes 1179656 | tf_op jit(solution)/shard_map/ppermute | solution.py:34
  109.7 2.5 %shard_map.162 = (bf16[32,6144]{1,0:T(8,128)(2,1)S(1)}, bf16[32,6144]{1,0:T(8,128)(2,1)}, bf16[32,6144]{1,0:T(8,128)(2,1)S(1)}, bf16[32,6144]{1,0:T(8,128)(2,1)S(1)}, bf16[32,6144]{1,0:T(8,128)(2,1)S(1)}) custom-call(bf16[256,640]{1,0:T(8,128)(2,1)S(1)} %get-tuple-element.31.active_ref, bf16[640,6144]{1,0:T(8,128)(2,1)S(1)} %shard_map.160.w_out_ref), custom_call_target="tpu_custom_call" | custom-call | flops 1258291200 | bytes 9830400 | tf_op jit(solution)/shard_map/pallas_call | solution.py:428
  112.2 2.7 %collective-permute-start.12 = (bf16[32,6144]{1,0:T(8,128)(2,1)S(1)}, bf16[32,6144]{1,0:T(8,128)(2,1)S(1)}, u32[]{:S(2)}, u32[]{:S(2)}) collective-permute-start(bf16[32,6144]{1,0:T(8,128)(2,1)S(1)} %get-tuple-element.34), channel_id=1, source_target_pairs={{0,96},{1,97},{2,98},{3,99},{4,100},{5,101},{6,102},{7,103},{8,104... | collective-permute-start | bytes 1179656 | tf_op jit(solution)/shard_map/ppermute | solution.py:34
  114.9 1.8 %collective-permute-done.15.refs_1_ = bf16[32,6144]{1,0:T(8,128)(2,1)S(1)} collective-permute-done((bf16[32,6144]{1,0:T(8,128)(2,1)S(1)}, bf16[32,6144]{1,0:T(8,128)(2,1)S(1)}, u32[]{:S(2)}, u32[]{:S(2)}) %collective-permute-start.15) | collective-permute-done | bytes 393248 | tf_op jit(solution)/shard_map/ppermute | solution.py:34
  117.9 2.8 %collective-permute-start.14 = (bf16[32,6144]{1,0:T(8,128)(2,1)S(1)}, bf16[32,6144]{1,0:T(8,128)(2,1)S(1)}, u32[]{:S(2)}, u32[]{:S(2)}) collective-permute-start(bf16[32,6144]{1,0:T(8,128)(2,1)S(1)} %shard_map.163), channel_id=1, source_target_pairs={{0,64},{1,65},{2,66},{3,67},{4,68},{5,69},{6,70},{7,71},{8,72},{9,... | collective-permute-start | bytes 1179656 | tf_op jit(solution)/shard_map/ppermute | solution.py:34
  121.4 3.7 %collective-permute-done.11.refs_1_ = bf16[32,6144]{1,0:T(8,128)(2,1)S(1)} collective-permute-done((bf16[32,6144]{1,0:T(8,128)(2,1)}, bf16[32,6144]{1,0:T(8,128)(2,1)S(1)}, u32[]{:S(2)}, u32[]{:S(2)}) %collective-permute-start.11) | collective-permute-done | bytes 393248 | tf_op jit(solution)/shard_map/ppermute | solution.py:34
  125.1 9.1 %collective-permute-done.14.refs_3_ = bf16[32,6144]{1,0:T(8,128)(2,1)S(1)} collective-permute-done((bf16[32,6144]{1,0:T(8,128)(2,1)S(1)}, bf16[32,6144]{1,0:T(8,128)(2,1)S(1)}, u32[]{:S(2)}, u32[]{:S(2)}) %collective-permute-start.14) | collective-permute-done | bytes 393248 | tf_op jit(solution)/shard_map/ppermute | solution.py:34
  135.2 7.4 %all-to-all-start.3 = ((bf16[16,2,6144]{2,1,0:T(2,128)(2,1)}), bf16[16,2,6144]{2,1,0:T(2,128)(2,1)S(1)}, u32[]{:S(2)}, u32[]{:S(2)}) async-start(bf16[16,2,6144]{2,1,0:T(2,128)(2,1)} %shard_map.165), calls=%async_computation.3 | async-start | bytes 786432 | tf_op jit(solution)/shard_map/all_to_all | solution.py:642
  142.8 9.7 %all-to-all-done.3 = bf16[16,2,6144]{2,1,0:T(2,128)(2,1)S(1)} async-done(((bf16[16,2,6144]{2,1,0:T(2,128)(2,1)}), bf16[16,2,6144]{2,1,0:T(2,128)(2,1)S(1)}, u32[]{:S(2)}, u32[]{:S(2)}) %all-to-all-start.3) | async-done | bytes 393248 | tf_op jit(solution)/shard_map/all_to_all | solution.py:642
  (92 shorter events, 27.5 us)
Async XLA Ops:
  0.0 57.2 %copy-start = (bf16[6144,16]{0,1:T(8,128)(2,1)S(1)}, bf16[6144,16]{0,1:T(8,128)(2,1)}, u32[]{:S(2)}) copy-start(bf16[6144,16]{0,1:T(8,128)(2,1)} %param.28) | copy-start | bytes 589828
  0.0 20.0 %collective-permute-start = (bf16[256,6144]{1,0:T(8,128)(2,1)}, bf16[256,6144]{1,0:T(8,128)(2,1)}, u32[]{:S(2)}, u32[]{:S(2)}) collective-permute-start(bf16[256,6144]{1,0:T(8,128)(2,1)} %own_ref.1), channel_id=1, source_target_pairs={{0,1},{1,0},{2,3},{3,2},{4,5},{5,4},{6,7},{7,6},{8,9},{9,8},{10,11... | collective-permute-start | bytes 9437192 | tf_op jit(solution)/shard_map/ppermute | solution.py:34
  3.1 13.2 %all-to-all-start = ((bf16[8,32,512]{2,1,0:T(8,128)(2,1)}), bf16[8,32,512]{2,1,0:T(8,128)(2,1)S(1)}, u32[]{:S(2)}, u32[]{:S(2)}) async-start(bf16[8,32,512]{2,1,0:T(8,128)(2,1)} %shard_map.154), calls=%async_computation | async-start | bytes 524288 | tf_op jit(solution)/shard_map/all_to_all | solution.py:561
  20.0 3.4 %collective-permute-start.2 = (bf16[64,640]{1,0:T(8,128)(2,1)S(1)}, bf16[64,640]{1,0:T(8,128)(2,1)S(1)}, u32[]{:S(2)}, u32[]{:S(2)}) collective-permute-start(bf16[64,640]{1,0:T(8,128)(2,1)S(1)} %shard_map.155), channel_id=1, source_target_pairs={{0,0},{1,1},{2,16},{3,17},{4,32},{5,33},{6,48},{7,49},{8,64},{9,65... | collective-permute-start | bytes 245768 | tf_op jit(solution)/shard_map/ppermute | solution.py:34
  22.8 19.4 %collective-permute-start.1 = (bf16[8,6272]{1,0:T(8,128)(2,1)S(1)}, bf16[8,6272]{1,0:T(8,128)(2,1)S(1)}, u32[]{:S(2)}, u32[]{:S(2)}) collective-permute-start(bf16[8,6272]{1,0:T(8,128)(2,1)S(1)} %fusion.6), channel_id=1, source_target_pairs={{0,0},{1,1},{2,16},{3,17},{4,32},{5,33},{6,48},{7,49},{8,64},{9,65... | collective-permute-start | bytes 301064 | tf_op jit(solution)/shard_map/ppermute | solution.py:34
  25.7 31.6 %copy-start.2 = (f32[6144]{0:T(1024)S(1)}, f32[6144]{0:T(1024)}, u32[]{:S(2)}) copy-start(f32[6144]{0:T(1024)} %param.27) | copy-start | bytes 73732
  25.7 31.0 %all-to-all-start.1 = ((bf16[8,8,6272]{2,1,0:T(8,128)(2,1)}), bf16[8,8,6272]{2,1,0:T(8,128)(2,1)S(1)}, u32[]{:S(2)}, u32[]{:S(2)}) async-start(bf16[8,8,6272]{2,1,0:T(8,128)(2,1)} %bitcast.13), calls=%async_computation.1 | async-start | bytes 1605632 | tf_op jit(solution)/shard_map/all_to_all | solution.py:582
  59.3 14.1 %all-to-all-start.2 = ((bf16[16,2,6144]{2,1,0:T(2,128)(2,1)}), bf16[16,2,6144]{2,1,0:T(2,128)(2,1)S(1)}, u32[]{:S(2)}, u32[]{:S(2)}) async-start(bf16[16,2,6144]{2,1,0:T(2,128)(2,1)} %reshape.276), calls=%async_computation.2 | async-start | bytes 786432 | tf_op jit(solution)/shard_map/all_to_all | solution.py:618
  63.6 15.1 %collective-permute-start.7 = (bf16[8,6272]{1,0:T(8,128)(2,1)S(1)}, bf16[8,6272]{1,0:T(8,128)(2,1)S(1)}, u32[]{:S(2)}, u32[]{:S(2)}) collective-permute-start(bf16[8,6272]{1,0:T(8,128)(2,1)S(1)} %pad_maximum_fusion.1), channel_id=1, source_target_pairs={{0,0},{1,1},{2,16},{3,17},{4,32},{5,33},{6,48},{7,49},{8,64},{9,65... | collective-permute-start | bytes 301064 | tf_op jit(solution)/shard_map/ppermute | solution.py:34
  73.5 6.9 %collective-permute-start.5 = (bf16[32,6144]{1,0:T(8,128)(2,1)S(1)}, bf16[32,6144]{1,0:T(8,128)(2,1)S(1)}, u32[]{:S(2)}, u32[]{:S(2)}) collective-permute-start(bf16[32,6144]{1,0:T(8,128)(2,1)S(1)} %reshape.277), channel_id=1, source_target_pairs={{0,16},{1,17},{2,18},{3,19},{4,20},{5,21},{6,22},{7,23},{8,24},{9,... | collective-permute-start | bytes 1179656 | tf_op jit(solution)/shard_map/ppermute | solution.py:34
  73.6 8.6 %collective-permute-start.6 = (bf16[32,6144]{1,0:T(8,128)(2,1)S(1)}, bf16[32,6144]{1,0:T(8,128)(2,1)S(1)}, u32[]{:S(2)}, u32[]{:S(2)}) collective-permute-start(bf16[32,6144]{1,0:T(8,128)(2,1)S(1)} %reshape.277), channel_id=1, source_target_pairs={{0,64},{1,65},{2,66},{3,67},{4,68},{5,69},{6,70},{7,71},{8,72},{9,... | collective-permute-start | bytes 1179656 | tf_op jit(solution)/shard_map/ppermute | solution.py:34
  73.7 18.8 %collective-permute-start.3 = (bf16[32,6144]{1,0:T(8,128)(2,1)S(1)}, bf16[32,6144]{1,0:T(8,128)(2,1)S(1)}, u32[]{:S(2)}, u32[]{:S(2)}) collective-permute-start(bf16[32,6144]{1,0:T(8,128)(2,1)S(1)} %reshape.277), channel_id=1, source_target_pairs={{0,96},{1,97},{2,98},{3,99},{4,100},{5,101},{6,102},{7,103},{8,104... | collective-permute-start | bytes 1179656 | tf_op jit(solution)/shard_map/ppermute | solution.py:34
  74.9 19.5 %collective-permute-start.4 = (bf16[32,6144]{1,0:T(8,128)(2,1)S(1)}, bf16[32,6144]{1,0:T(8,128)(2,1)S(1)}, u32[]{:S(2)}, u32[]{:S(2)}) collective-permute-start(bf16[32,6144]{1,0:T(8,128)(2,1)S(1)} %reshape.277), channel_id=1, source_target_pairs={{0,32},{1,33},{2,34},{3,35},{4,36},{5,37},{6,38},{7,39},{8,40},{9,... | collective-permute-start | bytes 1179656 | tf_op jit(solution)/shard_map/ppermute | solution.py:34
  82.2 18.8 %collective-permute-start.8 = (bf16[32,6144]{1,0:T(8,128)(2,1)S(1)}, bf16[32,6144]{1,0:T(8,128)(2,1)S(1)}, u32[]{:S(2)}, u32[]{:S(2)}) collective-permute-start(bf16[32,6144]{1,0:T(8,128)(2,1)S(1)} %collective-permute-done.5), channel_id=1, source_target_pairs={{0,96},{1,97},{2,98},{3,99},{4,100},{5,101},{6,102},{7,103},{8,104... | collective-permute-start | bytes 1179656 | tf_op jit(solution)/shard_map/ppermute | solution.py:34
  86.5 16.1 %collective-permute-start.9 = (bf16[32,6144]{1,0:T(8,128)(2,1)S(1)}, bf16[32,6144]{1,0:T(8,128)(2,1)S(1)}, u32[]{:S(2)}, u32[]{:S(2)}) collective-permute-start(bf16[32,6144]{1,0:T(8,128)(2,1)S(1)} %collective-permute-done.5), channel_id=1, source_target_pairs={{0,32},{1,33},{2,34},{3,35},{4,36},{5,37},{6,38},{7,39},{8,40},{9,... | collective-permute-start | bytes 1179656 | tf_op jit(solution)/shard_map/ppermute | solution.py:34
  86.5 13.2 %collective-permute-start.10 = (bf16[32,6144]{1,0:T(8,128)(2,1)S(1)}, bf16[32,6144]{1,0:T(8,128)(2,1)S(1)}, u32[]{:S(2)}, u32[]{:S(2)}) collective-permute-start(bf16[32,6144]{1,0:T(8,128)(2,1)S(1)} %collective-permute-done.6), channel_id=1, source_target_pairs={{0,16},{1,17},{2,18},{3,19},{4,20},{5,21},{6,22},{7,23},{8,24},{9,... | collective-permute-start | bytes 1179656 | tf_op jit(solution)/shard_map/ppermute | solution.py:34
  105.7 11.0 %collective-permute-start.15 = (bf16[32,6144]{1,0:T(8,128)(2,1)S(1)}, bf16[32,6144]{1,0:T(8,128)(2,1)S(1)}, u32[]{:S(2)}, u32[]{:S(2)}) collective-permute-start(bf16[32,6144]{1,0:T(8,128)(2,1)S(1)} %get-tuple-element.38), channel_id=1, source_target_pairs={{0,32},{1,33},{2,34},{3,35},{4,36},{5,37},{6,38},{7,39},{8,40},{9,... | collective-permute-start | bytes 1179656 | tf_op jit(solution)/shard_map/ppermute | solution.py:34
  106.0 10.7 %collective-permute-start.16 = (bf16[32,6144]{1,0:T(8,128)(2,1)S(1)}, bf16[32,6144]{1,0:T(8,128)(2,1)S(1)}, u32[]{:S(2)}, u32[]{:S(2)}) collective-permute-start(bf16[32,6144]{1,0:T(8,128)(2,1)S(1)} %get-tuple-element.39), channel_id=1, source_target_pairs={{0,96},{1,97},{2,98},{3,99},{4,100},{5,101},{6,102},{7,103},{8,104... | collective-permute-start | bytes 1179656 | tf_op jit(solution)/shard_map/ppermute | solution.py:34
  108.6 9.1 %collective-permute-start.13 = (bf16[32,6144]{1,0:T(8,128)(2,1)S(1)}, bf16[32,6144]{1,0:T(8,128)(2,1)S(1)}, u32[]{:S(2)}, u32[]{:S(2)}) collective-permute-start(bf16[32,6144]{1,0:T(8,128)(2,1)S(1)} %get-tuple-element.36), channel_id=1, source_target_pairs={{0,16},{1,17},{2,18},{3,19},{4,20},{5,21},{6,22},{7,23},{8,24},{9,... | collective-permute-start | bytes 1179656 | tf_op jit(solution)/shard_map/ppermute | solution.py:34
  112.2 12.9 %collective-permute-start.11 = (bf16[32,6144]{1,0:T(8,128)(2,1)}, bf16[32,6144]{1,0:T(8,128)(2,1)S(1)}, u32[]{:S(2)}, u32[]{:S(2)}) collective-permute-start(bf16[32,6144]{1,0:T(8,128)(2,1)} %get-tuple-element.33), channel_id=1, source_target_pairs={{0,32},{1,33},{2,34},{3,35},{4,36},{5,37},{6,38},{7,39},{8,40},{9,... | collective-permute-start | bytes 1179656 | tf_op jit(solution)/shard_map/ppermute | solution.py:34
  112.2 12.9 %collective-permute-start.12 = (bf16[32,6144]{1,0:T(8,128)(2,1)S(1)}, bf16[32,6144]{1,0:T(8,128)(2,1)S(1)}, u32[]{:S(2)}, u32[]{:S(2)}) collective-permute-start(bf16[32,6144]{1,0:T(8,128)(2,1)S(1)} %get-tuple-element.34), channel_id=1, source_target_pairs={{0,96},{1,97},{2,98},{3,99},{4,100},{5,101},{6,102},{7,103},{8,104... | collective-permute-start | bytes 1179656 | tf_op jit(solution)/shard_map/ppermute | solution.py:34
  116.8 8.3 %collective-permute-start.17 = (bf16[32,6144]{1,0:T(8,128)(2,1)S(1)}, bf16[32,6144]{1,0:T(8,128)(2,1)S(1)}, u32[]{:S(2)}, u32[]{:S(2)}) collective-permute-start(bf16[32,6144]{1,0:T(8,128)(2,1)S(1)} %shard_map.164), channel_id=1, source_target_pairs={{0,16},{1,17},{2,18},{3,19},{4,20},{5,21},{6,22},{7,23},{8,24},{9,... | collective-permute-start | bytes 1179656 | tf_op jit(solution)/shard_map/ppermute | solution.py:34
  117.9 16.4 %collective-permute-start.14 = (bf16[32,6144]{1,0:T(8,128)(2,1)S(1)}, bf16[32,6144]{1,0:T(8,128)(2,1)S(1)}, u32[]{:S(2)}, u32[]{:S(2)}) collective-permute-start(bf16[32,6144]{1,0:T(8,128)(2,1)S(1)} %shard_map.163), channel_id=1, source_target_pairs={{0,64},{1,65},{2,66},{3,67},{4,68},{5,69},{6,70},{7,71},{8,72},{9,... | collective-permute-start | bytes 1179656 | tf_op jit(solution)/shard_map/ppermute | solution.py:34
  135.2 17.2 %all-to-all-start.3 = ((bf16[16,2,6144]{2,1,0:T(2,128)(2,1)}), bf16[16,2,6144]{2,1,0:T(2,128)(2,1)S(1)}, u32[]{:S(2)}, u32[]{:S(2)}) async-start(bf16[16,2,6144]{2,1,0:T(2,128)(2,1)} %shard_map.165), calls=%async_computation.3 | async-start | bytes 786432 | tf_op jit(solution)/shard_map/all_to_all | solution.py:642
  (2 other events, 11.3 us)
